TPU v7x, 32 devices: a whole 2x2x4 slice. The times are simulated.
32 devices in a mesh: sa: 4 (over z), sb: 4 (over y, core), sl: 2 (over x).
Axes of the slice: x: 2, y: 2, z: 4, core: 2. Of those that a mesh axis runs over, the one named last changes fastest.
Arguments:
- stem_cache: bfloat16 [32, 2, 128, 4096], P(('sa', 'sb', 'sl')), may hold values from -6 to 6
- subtree_cache: bfloat16 [32, 2, 4096, 512], P(('sa', 'sb', 'sl')), may hold values from -0.0625 to 0.0625
- final_gates: bfloat16 [2, 512, 512], replicated, may hold values from -0.03125 to 0.03125
- group_rows: int32 [32], replicated, may hold values from 0 to 7
Outputs:
- amplitudes: float32 [512, 1024], P(('sa', 'sb', 'sl'))
All inputs are finite; a program needn't handle non-finite values.
Results may differ from a plain program's by a relative error of at most 0.0029.
Values may be sent and summed in bfloat16 or wider, within the bound.
A program may use at most 64 MiB of HBM per device.

v0:
```python
import jax
import jax.numpy as jnp
from jax import lax
from jax.sharding import PartitionSpec as P

RB = 16


def swapped(shard, axis, apart):
    return lax.ppermute(shard, axis, [(i, i ^ 1 << apart) for i in range(lax.axis_size(axis))])


def complex_dot(left_real, left_imag, right):
    real = jnp.dot(left_real, right[0], preferred_element_type=jnp.float32) - jnp.dot(
        left_imag, right[1], preferred_element_type=jnp.float32
    )
    imag = jnp.dot(left_real, right[1], preferred_element_type=jnp.float32) + jnp.dot(
        left_imag, right[0], preferred_element_type=jnp.float32
    )
    return (real, imag)


def local(stem_cache, subtree_cache, final_gates, group_rows):
    stem = stem_cache[0]
    half = stem.shape[1] // 2
    upper = swapped(stem[:, half:], "sb", 0)
    whole = jnp.concatenate([stem[:, :half], upper], axis=1)
    top_bit = lax.axis_size("sa").bit_length() - 2
    subtree = subtree_cache[0]
    left = swapped(whole, "sa", top_bit)
    real, imag = complex_dot(left[0], left[1], subtree)
    partial_s = jnp.stack([real, imag]).astype(jnp.bfloat16)
    total_rows = group_rows.shape[0] * RB
    group_count = total_rows // lax.axis_size(("sa", "sb"))
    rows = jnp.arange(group_count * lax.axis_size(("sa", "sb")), dtype=jnp.int32)
    chosen = jnp.take(partial_s, jnp.take(group_rows, rows // RB) * RB + rows % RB, axis=1)
    out_real, out_imag = complex_dot(chosen[0], chosen[1], final_gates)
    outer = lax.psum_scatter(
        jnp.concatenate([out_real, out_imag], axis=1), ("sa", "sb"), scatter_dimension=0, tiled=True
    )
    amplitudes = lax.psum_scatter(outer, "sl", scatter_dimension=0, tiled=True)
    return amplitudes


def solution(mesh):
    return jax.shard_map(
        local,
        mesh=mesh,
        in_specs=(
            P(("sa", "sb", "sl"), None, None, None),
            P(("sa", "sb", "sl"), None, None, None),
            P(),
            P(),
        ),
        out_specs=P(("sa", "sb", "sl"), None),
        check_vma=False,
    )
```

profile of v0, /device:TPU:0, one launch (start us, length us, event | category | flops | bytes accessed | tf_op | source)
XLA Modules:
  0.0 202.0 jit_solution(8393926224540243176)
XLA Ops:
  6.5 0.0 reduce-scatter.7.cloned.1.call-start
  6.5 0.0 copy-start.1
  6.5 0.0 copy-start.2
  6.5 1.9 fusion.58
  8.4 0.5 collective-permute-start
  9.0 2.3 %collective-permute-done = bf16[2,64,4096]{2,1,0:T(8,128)(2,1)S(1)} collective-permute-done((bf16[2,64,4096]{2,1,0:T(8,128)(2,1)S(1)}, bf16[2,64,4096]{2,1,0:T(8,128)(2,1)S(1)}, u32[]{:S(2)}, u32[]{:S(2)}) %collective-permute-start) | collective-permute-done | bytes 1048608 | tf_op jit(solution)/shard_map/ppermute | solution.py:10
  11.3 0.2 pad_maximum_fusion
  11.5 4.0 %collective-permute-start.1 = (bf16[2,128,4096]{2,1,0:T(8,128)(2,1)S(1)}, bf16[2,128,4096]{2,1,0:T(8,128)(2,1)S(1)}, u32[]{:S(2)}, u32[]{:S(2)}) collective-permute-start(bf16[2,128,4096]{2,1,0:T(8,128)(2,1)S(1)} %pad_maximum_fusion), channel_id=1, source_target_pairs={{0,16},{8,24},{16,0},{24,8},{1,17},{9,25},{17,1},{25,9},{2,18},{10... | collective-permute-start | bytes 6291464 | tf_op jit(solution)/shard_map/ppermute | solution.py:10
  16.4 0.0 copy-done.1
  16.4 0.7 fusion.61
  17.1 4.4 %compare_select_fusion.2 = s32[512,1]{0,1:T(1,128)S(1)} fusion(s32[]{:T(128)} %bitcast.25, s32[]{:T(128)} %bitcast.26, s32[]{:T(128)} %bitcast.27, s32[]{:T(128)} %bitcast.28, s32[]{:T(128)} %bitcast.29, s32[]{:T(128)} %bitcast.31, s32[]{:T(128)} %bitcast.30), kind=kLoop, calls=%fused_computation.73 | loop fusion | flops 11776 | bytes 2076 | tf_op jit(solution)/shard_map/jit(_take)/gather | solution.py:36
  21.5 0.7 fusion.60
  22.2 15.6 %compare_and_fusion = (pred[512]{0:T(512)(128)(4,1)S(1)}, s32[512]{0:T(512)S(1)}) fusion(pred[512]{0:T(512)(128)(4,1)S(1)} %compare_reduce_fusion, pred[512]{0:T(512)(128)(4,1)S(1)} %compare_reduce_fusion.1, pred[512]{0:T(512)(128)(4,1)S(1)} %compare_reduce_fusion.2, pred[512]{0:T(512)(128)(4,1)S(1)} %compare_reduce_fusion.3, ...), kind=kLoop, calls=%fused_computation.102 | loop fusion | flops 26624 | bytes 17508 | tf_op jit(solution)/shard_map/jit(_take)/and | solution.py:36
  37.8 68.6 %collective-permute-done.1 = bf16[2,128,4096]{2,1,0:T(8,128)(2,1)S(1)} collective-permute-done((bf16[2,128,4096]{2,1,0:T(8,128)(2,1)S(1)}, bf16[2,128,4096]{2,1,0:T(8,128)(2,1)S(1)}, u32[]{:S(2)}, u32[]{:S(2)}) %collective-permute-start.1) | collective-permute-done | bytes 2097184 | tf_op jit(solution)/shard_map/ppermute | solution.py:10
  106.4 0.0 copy-done.2
  106.4 0.7 fusion.4
  107.1 0.7 fusion.2
  107.8 0.7 fusion.27
  108.5 0.7 fusion.24
  109.3 0.3 copy.10
  109.6 0.0 copy-start
  109.6 3.6 %gather_fusion = bf16[512,2,512]{2,1,0:T(2,128)(2,1)S(1)} fusion(bf16[2,128,512]{2,0,1:T(2,128)(2,1)S(1)} %copy.10, s32[1024]{0:T(1024)S(1)} %pad_clamp_fusion), kind=kCustom, calls=%fused_computation | custom fusion | bytes 2099200 | tf_op jit(solution)/shard_map/jit(_take)/gather | solution.py:36
  113.2 2.0 fusion.30
  115.1 1.5 fusion.59
  116.6 0.0 copy-done
  116.7 0.5 fusion.33
  117.2 0.5 fusion.35
  117.6 0.5 convolution_add_fusion
  118.1 0.5 convolution_subtract_fusion
  118.6 0.2 pad_maximum_fusion.1
  118.8 1.9 copy.12
  120.7 0.0 reduce-scatter.7.cloned.1.call-update
  120.7 0.0 reduce-scatter.9.cloned.1.call-start
  120.8 62.9 %reduce-scatter.7.cloned.1.call-done = f32[32,1024]{1,0:T(8,128)} async-done(((f32[512,1024]{1,0:T(8,128)}), f32[32,1024]{1,0:T(8,128)}) %reduce-scatter.7.cloned.1.call-update) | async-done | bytes 131088
  183.6 0.0 reduce-scatter.9.cloned.1.call-update
  183.6 11.5 %reduce-scatter.9.cloned.1.call-done = f32[16,1024]{1,0:T(8,128)} async-done(((f32[32,1024]{1,0:T(8,128)}), f32[16,1024]{1,0:T(8,128)}) %reduce-scatter.9.cloned.1.call-update) | async-done | bytes 65552 | tf_op jit(solution)/shard_map/reduce_scatter | solution.py:41
  (28 shorter events, 0.9 us)
Async XLA Ops:
  6.5 177.1 %reduce-scatter.7.cloned.1.call-start = ((), (), s32[]{:S(2)}) async-start(), calls=%async_computation.2 | async-start | bytes 2228224
  6.5 9.8 %copy-start.1 = (s32[32]{0:T(128)S(1)}, s32[32]{0:T(128)}, u32[]{:S(2)}) copy-start(s32[32]{0:T(128)} %param.7) | copy-start | bytes 388
  6.5 99.8 %copy-start.2 = (bf16[1,2,4096,512]{3,2,1,0:T(8,128)(2,1)S(1)}, bf16[1,2,4096,512]{3,2,1,0:T(8,128)(2,1)}, u32[]{:S(2)}) copy-start(bf16[1,2,4096,512]{3,2,1,0:T(8,128)(2,1)} %param.5) | copy-start | bytes 25165828
  8.4 2.8 %collective-permute-start = (bf16[2,64,4096]{2,1,0:T(8,128)(2,1)S(1)}, bf16[2,64,4096]{2,1,0:T(8,128)(2,1)S(1)}, u32[]{:S(2)}, u32[]{:S(2)}) collective-permute-start(bf16[2,64,4096]{2,1,0:T(8,128)(2,1)S(1)} %get-tuple-element.8), channel_id=1, source_target_pairs={{0,2},{2,0},{4,6},{6,4},{1,3},{3,1},{5,7},{7,5},{8,10},{10,8},{12,... | collective-permute-start | bytes 3145736 | tf_op jit(solution)/shard_map/ppermute | solution.py:10
  11.5 94.9 %collective-permute-start.1 = (bf16[2,128,4096]{2,1,0:T(8,128)(2,1)S(1)}, bf16[2,128,4096]{2,1,0:T(8,128)(2,1)S(1)}, u32[]{:S(2)}, u32[]{:S(2)}) collective-permute-start(bf16[2,128,4096]{2,1,0:T(8,128)(2,1)S(1)} %pad_maximum_fusion), channel_id=1, source_target_pairs={{0,16},{8,24},{16,0},{24,8},{1,17},{9,25},{17,1},{25,9},{2,18},{10... | collective-permute-start | bytes 6291464 | tf_op jit(solution)/shard_map/ppermute | solution.py:10
  109.6 7.1 %copy-start = (bf16[2,512,512]{2,1,0:T(8,128)(2,1)S(1)}, bf16[2,512,512]{2,1,0:T(8,128)(2,1)}, u32[]{:S(2)}) copy-start(bf16[2,512,512]{2,1,0:T(8,128)(2,1)} %param.6) | copy-start | bytes 3145732
  120.7 74.5 %reduce-scatter.9.cloned.1.call-start = ((), (), s32[]{:S(2)}) async-start(), calls=%async_computation.3 | async-start | bytes 196608 | tf_op jit(solution)/shard_map/reduce_scatter | solution.py:41
Sparse Core Ops, SparseCore 0:
  120.8 62.7 reduce-scatter.6
  185.9 9.2 reduce-scatter.8
where the time goes:
time: 202 us
  waiting for transfers between devices  145 us (72%)
  other arithmetic  23.2 us (11%)
  between operations  13.6 us (7%)
  local copies, waits for them, and re-layouts  10.6 us (5%)
  matrix products  4.82 us (2%)
  starting transfers between devices  4.58 us (2%)
    ppermute x2, waiting for transfers between devices, swapped(): lax.ppermute(shard, axis, [(i, i ^ 1 << apart) for i in range(lax.axis_si...  70.8 us
    unnamed x3, waiting for transfers between devices  62.9 us
    and x1, other arithmetic, local(): jnp.take(partial_s, jnp.take(group_rows, rows // RB) * RB + rows % RB, ax...  15.6 us
    reduce_scatter x1, waiting for transfers between devices, local(): amplitudes = lax.psum_scatter(outer, 'sl', scatter_dimension=0, tiled=True)  11.5 us
    gather x26, other arithmetic, local(): jnp.take(group_rows, rows // RB) * RB + rows % RB  5.23 us
    ppermute x2, starting transfers between devices, swapped(): lax.ppermute(shard, axis, [(i, i ^ 1 << apart) for i in range(lax.axis_si...  4.54 us
  transfers between devices with their start and end apart: 4, of which 4 were waited for; matrix products, arithmetic and copies ran while one was open for 11% of the time, Pallas kernels for 0%

commit v1 on v0

v1 whole, which is shorter than its diff:
```python
import functools

import jax
import jax.numpy as jnp
from jax import lax
from jax.experimental import pallas as pl
from jax.experimental.pallas import tpu as pltpu
from jax.sharding import PartitionSpec as P

RB = 16
AXES = ("sa", "sb", "sl")
STAGE = 2 * RB
LANES = 128
MESH = pl.DeviceIdType.MESH


def kernel(n_sa, n_sb, n_sl, row_groups, stem, subtree, gates, group_rows, out, held, sub, gate, part, rs, zb, ag,
           sub_sem, gate_sem, stem_send, stem_recv, rs_send, rs_recv, z_send, z_recv, ag_send, ag_recv):
    sa, sb, sl = (lax.axis_index(a) for a in AXES)
    stages = held.shape[0]
    n = subtree.shape[2]
    owners = 4 * n_sb
    per_half = owners // 2
    me = (sa % 2) * (2 * n_sb) + sb * 2 + sl % 2
    others = (n_sa // 2) * (n_sl // 2)
    my_q = (sa // 2) * (n_sl // 2) + sl // 2

    def owner_device(o):
        return ((sa // 2) * 2 + o // (2 * n_sb), (o // 2) % n_sb, (sl // 2) * 2 + o % 2)

    def other_device(q):
        return ((q // (n_sl // 2)) * 2 + sa % 2, sb, (q % (n_sl // 2)) * 2 + sl % 2)

    far = lax.rem(sa + n_sa // 2, n_sa)
    pair = sb + 1 - 2 * (sb % 2)

    pltpu.make_async_copy(subtree, sub, sub_sem).start()
    pltpu.make_async_copy(gates, gate, gate_sem).start()

    barrier = pltpu.get_barrier_semaphore()
    for b in (sb, pair):
        pl.semaphore_signal(barrier, inc=1, device_id=(far, b, sl), device_id_type=MESH)

    @pl.loop(1, owners)
    def _(j):
        pl.semaphore_signal(barrier, inc=1, device_id=owner_device((me + j) % owners), device_id_type=MESH)

    @pl.loop(1, others)
    def _(j):
        pl.semaphore_signal(barrier, inc=1, device_id=other_device((my_q + j) % others), device_id_type=MESH)

    pl.semaphore_wait(barrier, 2 + (owners - 1) + (others - 1))

    def stem_copy(t):
        target = sb if t < stages // 2 else pair
        return pltpu.make_async_remote_copy(
            src_ref=stem.at[:, pl.ds(t * STAGE, STAGE), :], dst_ref=held.at[t], send_sem=stem_send.at[t],
            recv_sem=stem_recv.at[t], device_id=(far, target, sl), device_id_type=MESH)

    def rs_copy(t, to, slot):
        return pltpu.make_async_remote_copy(
            src_ref=part.at[t, to], dst_ref=rs.at[t, slot], send_sem=rs_send.at[t, to],
            recv_sem=rs_recv.at[t, slot], device_id=owner_device(to), device_id_type=MESH)

    def z_copy(t, to, slot):
        return pltpu.make_async_remote_copy(
            src_ref=zb.at[t, slot], dst_ref=zb.at[t, slot], send_sem=z_send.at[t, to],
            recv_sem=z_recv.at[t, slot], device_id=other_device(to), device_id_type=MESH)

    def ag_copy(t, to, slot):
        piece = ag.at[2 * t + slot // per_half, slot % per_half]
        return pltpu.make_async_remote_copy(
            src_ref=piece, dst_ref=piece, send_sem=ag_send.at[t, to],
            recv_sem=ag_recv.at[t, slot], device_id=owner_device(to), device_id_type=MESH)

    for t in range(stages):
        stem_copy(t).start()
    pltpu.make_async_copy(subtree, sub, sub_sem).wait()
    pltpu.make_async_copy(gates, gate, gate_sem).wait()

    for t in range(stages):
        stem_copy(t).wait_recv()

        @functools.partial(lax.fori_loop, 0, 2, init_val=0)
        def _(i, carry, t=t):
            cols = pl.ds(pl.multiple_of(i * (n // 2), n // 2), n // 2)
            left = held[t].reshape(2 * STAGE, held.shape[3])
            by_real = jnp.dot(left, sub[0, :, cols], preferred_element_type=jnp.float32)
            by_imag = jnp.dot(left, sub[1, :, cols], preferred_element_type=jnp.float32)
            real = (by_real[:STAGE] - by_imag[STAGE:]).astype(jnp.bfloat16)
            imag = (by_imag[:STAGE] + by_real[STAGE:]).astype(jnp.bfloat16)
            pieces = n // 2 // LANES
            for half in range(2):
                for p in range(pieces):
                    at = half * per_half + i * pieces + p
                    block = (slice(half * RB, (half + 1) * RB), slice(p * LANES, (p + 1) * LANES))
                    part[t, at] = real[block]
                    part[t, at + per_half // 2] = imag[block]
            return carry

        @pl.loop(1, owners)
        def _(j):
            rs_copy(t, (me + j) % owners, me).start()

        rs[t, me] = part[t, me]

        @pl.loop(1, owners)
        def _(j):
            rs_copy(t, (me + j) % owners, (me + j) % owners).wait_recv()

        zb[t, my_q] = jnp.sum(rs[t].astype(jnp.float32), axis=0)

        @pl.loop(1, others)
        def _(j):
            z_copy(t, (my_q + j) % others, my_q).start()

        @pl.loop(1, others)
        def _(j):
            z_copy(t, (my_q + j) % others, (my_q + j) % others).wait_recv()

        ag[2 * t + me // per_half, me % per_half] = jnp.sum(zb[t], axis=0)

        @pl.loop(1, owners)
        def _(j):
            ag_copy(t, (me + j) % owners, me).start()

    for t in range(stages):
        stem_copy(t).wait_send()

        @pl.loop(1, owners)
        def _(j):
            rs_copy(t, (me + j) % owners, me).wait_send()

        @pl.loop(1, others)
        def _(j):
            z_copy(t, (my_q + j) % others, my_q).wait_send()

        @pl.loop(1, owners)
        def _(j):
            ag_copy(t, (me + j) % owners, (me + j) % owners).wait_recv()

        @pl.loop(1, owners)
        def _(j):
            ag_copy(t, (me + j) % owners, me).wait_send()

    device = (sa * n_sb + sb) * n_sl + sl
    block = ag[group_rows[device // row_groups]]
    rows = jnp.concatenate([block[p] for p in range(per_half)], axis=1)
    high = rows.astype(jnp.bfloat16)
    rest = rows - high.astype(jnp.float32)
    middle = rest.astype(jnp.bfloat16)
    low = (rest - middle.astype(jnp.float32)).astype(jnp.bfloat16)
    thirds = jnp.concatenate([low, middle, high], axis=0)

    def times(k, g):
        x = jnp.dot(thirds[:, k * n:(k + 1) * n], gate[g], preferred_element_type=jnp.float32)
        return x[:RB] + x[RB:2 * RB] + x[2 * RB:]

    out[:, :n] = times(0, 0) - times(1, 1)
    out[:, n:] = times(0, 1) + times(1, 0)


def local(stem_cache, subtree_cache, final_gates, group_rows):
    stem, subtree = stem_cache[0], subtree_cache[0]
    n_sa, n_sb, n_sl = (lax.axis_size(a) for a in AXES)
    m, k = stem.shape[1:]
    n = subtree.shape[2]
    stages = m // STAGE
    owners = 4 * n_sb
    others = (n_sa // 2) * (n_sl // 2)
    count = n_sa * n_sb * n_sl
    out_rows = group_rows.shape[0] * RB // count
    dma = pltpu.SemaphoreType.DMA
    block = pl.pallas_call(
        functools.partial(kernel, n_sa, n_sb, n_sl, RB // out_rows),
        out_shape=jax.ShapeDtypeStruct((RB, 2 * n), jnp.float32),
        in_specs=[pl.BlockSpec(memory_space=pl.ANY)] * 3 + [pl.BlockSpec(memory_space=pltpu.SMEM)],
        out_specs=pl.BlockSpec(memory_space=pltpu.VMEM),
        scratch_shapes=[
            pltpu.VMEM((stages, 2, STAGE, k), jnp.bfloat16),
            pltpu.VMEM((2, k, n), jnp.bfloat16),
            pltpu.VMEM((2, n, n), jnp.bfloat16),
            pltpu.VMEM((stages, owners, RB, LANES), jnp.bfloat16),
            pltpu.VMEM((stages, owners, RB, LANES), jnp.bfloat16),
            pltpu.VMEM((stages, others, RB, LANES), jnp.float32),
            pltpu.VMEM((2 * stages, owners // 2, RB, LANES), jnp.float32),
            dma, dma, dma((stages,)), dma((stages,)),
            dma((stages, owners)), dma((stages, owners)),
            dma((stages, others)), dma((stages, others)),
            dma((stages, owners)), dma((stages, owners)),
        ],
        compiler_params=pltpu.CompilerParams(
            collective_id=0, has_side_effects=True, vmem_limit_bytes=40 * 1024 * 1024
        ),
    )(stem, subtree, final_gates, group_rows)
    if out_rows == RB:
        return block
    return lax.dynamic_slice_in_dim(block, lax.axis_index(AXES) * out_rows % RB, out_rows, axis=0)


def solution(mesh):
    return jax.shard_map(
        local,
        mesh=mesh,
        in_specs=(
            P(AXES, None, None, None),
            P(AXES, None, None, None),
            P(),
            P(),
        ),
        out_specs=P(AXES, None),
        check_vma=False,
    )
```

time: 202 us -> 139 us (0.69)
  waiting for transfers between devices: 145 us -> 0 us
  Pallas kernels: 0 us -> 131 us
  other arithmetic: 23.2 us -> 0 us
  between operations: 13.6 us -> 0.01 us
  matrix products: 4.82 us -> 0 us
  starting transfers between devices: 4.58 us -> 0 us
  local copies, waits for them, and re-layouts: 10.6 us -> 7.48 us
    pallas_call x0 -> x1, Pallas kernels: none -> 131 us  [local(): pl.pallas_call(functools.partial(kernel, n_sa, n_sb, n_sl, RB // out_rows...]
    ppermute x2 -> x0, waiting for transfers between devices: 70.8 us -> none  [swapped(): lax.ppermute(shard, axis, [(i, i ^ 1 << apart) for i in range(lax.axis_si...]
    unnamed x3 -> x0, waiting for transfers between devices: 62.9 us -> none
    and x1 -> x0, other arithmetic: 15.6 us -> none  [local(): jnp.take(partial_s, jnp.take(group_rows, rows // RB) * RB + rows % RB, ax...]
    reduce_scatter x1 -> x0, waiting for transfers between devices: 11.5 us -> none  [local(): amplitudes = lax.psum_scatter(outer, 'sl', scatter_dimension=0, tiled=True)]
    unnamed x7 -> x9, local copies, waits for them, and re-layouts: 1.89 us -> 7.48 us
    gather x27 -> x0, other arithmetic: 5.23 us -> none  [the longest x26 5.23 us: local(): jnp.take(group_rows, rows // RB) * RB + rows % RB]
    gather x3 -> x0, local copies, waits for them, and re-layouts: 5 us -> none  [the longest x1 3.56 us: local(): jnp.take(partial_s, jnp.take(group_rows, rows // RB) * RB + rows % RB, ax...]
  transfers between devices with their start and end apart: 4 -> 0, of which waited for: 4 -> 0; matrix products, arithmetic and copies ran while one was open for 11% -> 0% of each run, Pallas kernels for 0% -> 0%
where the time goes in v1:
time: 139 us
  Pallas kernels  131 us (94%)
  local copies, waits for them, and re-layouts  7.48 us (5%)
    pallas_call x1, Pallas kernels, local(): pl.pallas_call(functools.partial(kernel, n_sa, n_sb, n_sl, RB // out_rows...  131 us
    unnamed x9, local copies, waits for them, and re-layouts  7.48 us

profile of v1, /device:TPU:0, one launch (start us, length us, event | category | flops | bytes accessed | tf_op | source)
XLA Modules:
  0.0 138.9 jit_solution(3787871235335028861)
XLA Ops:
  0.0 0.0 copy-start
  0.0 3.4 %copy-done = bf16[1,2,4096,512]{3,2,1,0:T(8,128)(2,1)S(1)} copy-done((bf16[1,2,4096,512]{3,2,1,0:T(8,128)(2,1)S(1)}, bf16[1,2,4096,512]{3,2,1,0:T(8,128)(2,1)}, u32[]{:S(2)}) %copy-start) | copy-done | bytes 8388632
  3.4 0.0 copy-start.1
  3.4 1.6 %copy-done.1 = bf16[1,2,128,4096]{3,2,1,0:T(8,128)(2,1)S(1)} copy-done((bf16[1,2,128,4096]{3,2,1,0:T(8,128)(2,1)S(1)}, bf16[1,2,128,4096]{3,2,1,0:T(8,128)(2,1)}, u32[]{:S(2)}) %copy-start.1) | copy-done | bytes 2097176
  5.0 0.0 copy-start.2
  5.0 1.2 copy-done.2
  6.2 0.0 copy-start.3
  6.2 0.7 copy-done.3
  6.9 131.4 %shard_map.46 = f32[16,1024]{1,0:T(8,128)S(1)} custom-call(bf16[2,128,4096]{2,1,0:T(8,128)(2,1)S(1)} %bitcast.3, bf16[2,4096,512]{2,1,0:T(8,128)(2,1)S(1)} %bitcast.2, bf16[2,512,512]{2,1,0:T(8,128)(2,1)S(1)} %copy-done.2, s32[32]{0:T(128)S(1)} %copy-done.3), custom_call_target="tpu_custom_call" | custom-call | tf_op jit(solution)/shard_map/pallas_call | solution.py:174
  138.3 0.6 copy.6
Async XLA Ops:
  0.0 3.4 %copy-start = (bf16[1,2,4096,512]{3,2,1,0:T(8,128)(2,1)S(1)}, bf16[1,2,4096,512]{3,2,1,0:T(8,128)(2,1)}, u32[]{:S(2)}) copy-start(bf16[1,2,4096,512]{3,2,1,0:T(8,128)(2,1)} %param.5) | copy-start | bytes 25165828
  3.4 1.6 %copy-start.1 = (bf16[1,2,128,4096]{3,2,1,0:T(8,128)(2,1)S(1)}, bf16[1,2,128,4096]{3,2,1,0:T(8,128)(2,1)}, u32[]{:S(2)}) copy-start(bf16[1,2,128,4096]{3,2,1,0:T(8,128)(2,1)} %param.4) | copy-start | bytes 6291460
  5.0 1.2 copy-start.2
  6.2 0.7 copy-start.3

commit v2 on v1

v2 whole, which is shorter than its diff:
```python
import functools
import itertools

import jax
import jax.numpy as jnp
from jax import lax
from jax.experimental import pallas as pl
from jax.experimental.pallas import tpu as pltpu
from jax.sharding import PartitionSpec as P

RB = 16
AXES = ("sa", "sb", "sl")
STAGE = 2 * RB
LANES = 128
MESH = pl.DeviceIdType.MESH


def kernel(n_sa, n_sb, n_sl, row_groups, stem, subtree, gates, group_rows, out, held, sub, gate, part, rs, zb, ag,
           sub_sem, gate_sem, stem_send, stem_recv, rs_send, rs_recv, z_send, z_recv, ag_send, ag_recv):
    sa, sb, sl = (lax.axis_index(a) for a in AXES)
    stages = held.shape[0]
    n = subtree.shape[2]
    owners = 4 * n_sb
    per_half = owners // 2
    me = (sa % 2) * (2 * n_sb) + sb * 2 + sl % 2
    others = (n_sa // 2) * (n_sl // 2)
    my_q = (sa // 2) * (n_sl // 2) + sl // 2

    near_peers = []
    for da, db, dl in itertools.product((0, 1), range(n_sb), (0, 1)):
        if da or db or dl:
            a, b, l = (sa + da) % 2, (sb + db) % n_sb, (sl + dl) % 2
            near_peers.append((a * (2 * n_sb) + b * 2 + l, (sa - sa % 2 + a, b, sl - sl % 2 + l)))
    near_peers.reverse()
    far_peers = []
    for da, dl in itertools.product(range(n_sa // 2), range(n_sl // 2)):
        if da or dl:
            far_peers.append(((sa + 2 * da) % n_sa, sb, (sl + 2 * dl) % n_sl))

    far = lax.rem(sa + n_sa // 2, n_sa)
    pair = sb + 1 - 2 * (sb % 2)

    pltpu.make_async_copy(subtree, sub, sub_sem).start()
    pltpu.make_async_copy(gates, gate, gate_sem).start()

    barrier = pltpu.get_barrier_semaphore()
    for b in (sb, pair):
        pl.semaphore_signal(barrier, inc=1, device_id=(far, b, sl), device_id_type=MESH)

    for device in [d for _, d in near_peers] + far_peers:
        pl.semaphore_signal(barrier, inc=1, device_id=device, device_id_type=MESH)

    pl.semaphore_wait(barrier, 2 + (owners - 1) + (others - 1))

    def stem_copy(i):
        target = sb if i < stages else pair
        return pltpu.make_async_remote_copy(
            src_ref=stem.at[:, pl.ds(i * RB, RB), :], dst_ref=held.at[i // 2, :, pl.ds(i % 2 * RB, RB)],
            send_sem=stem_send.at[i], recv_sem=stem_recv.at[i], device_id=(far, target, sl), device_id_type=MESH)

    def rs_copy(t, peer):
        slot, device = peer
        return pltpu.make_async_remote_copy(
            src_ref=part.at[t, slot], dst_ref=rs.at[t, me], send_sem=rs_send.at[t],
            recv_sem=rs_recv.at[t], device_id=device, device_id_type=MESH)

    def z_copy(t, device):
        return pltpu.make_async_remote_copy(
            src_ref=zb.at[t, my_q], dst_ref=zb.at[t, my_q], send_sem=z_send.at[t],
            recv_sem=z_recv.at[t], device_id=device, device_id_type=MESH)

    def ag_copy(t, peer):
        piece = ag.at[t, me]
        return pltpu.make_async_remote_copy(
            src_ref=piece, dst_ref=piece, send_sem=ag_send.at[t],
            recv_sem=ag_recv.at[t], device_id=peer[1], device_id_type=MESH)

    def wait_all(buffer, t, count, sem):
        if count:
            block = buffer.at[t, pl.ds(0, count)]
            pltpu.make_async_copy(block, block, sem.at[t]).wait()

    for i in range(2):
        stem_copy(i).start()
    pltpu.make_async_copy(subtree, sub, sub_sem).wait()
    pltpu.make_async_copy(gates, gate, gate_sem).wait()

    for t in range(stages):
        for i in (2 * t, 2 * t + 1):
            stem_copy(i).wait_send()
            if i + 2 < 2 * stages:
                stem_copy(i + 2).start()
        for i in (2 * t, 2 * t + 1):
            stem_copy(i).wait_recv()

        @functools.partial(lax.fori_loop, 0, 2, init_val=0)
        def _(i, carry, t=t):
            cols = pl.ds(pl.multiple_of(i * (n // 2), n // 2), n // 2)
            left = held[t].reshape(2 * STAGE, held.shape[3])
            by_real = jnp.dot(left, sub[0, :, cols], preferred_element_type=jnp.float32)
            by_imag = jnp.dot(left, sub[1, :, cols], preferred_element_type=jnp.float32)
            real = (by_real[:STAGE] - by_imag[STAGE:]).astype(jnp.bfloat16)
            imag = (by_imag[:STAGE] + by_real[STAGE:]).astype(jnp.bfloat16)
            pieces = n // 2 // LANES
            for half in range(2):
                for p in range(pieces):
                    at = half * per_half + i * pieces + p
                    block = (slice(half * RB, (half + 1) * RB), slice(p * LANES, (p + 1) * LANES))
                    part[t, at] = real[block]
                    part[t, at + per_half // 2] = imag[block]
            return carry

        for peer in near_peers:
            rs_copy(t, peer).start()

        rs[t, me] = part[t, me]

        wait_all(rs, t, owners - 1, rs_recv)

        zb[t, my_q] = jnp.sum(rs[t].astype(jnp.float32), axis=0)

        for device in far_peers:
            z_copy(t, device).start()

        wait_all(zb, t, others - 1, z_recv)

        ag[t, me] = jnp.sum(zb[t], axis=0)

        for peer in near_peers:
            ag_copy(t, peer).start()

    for t in range(stages):

        wait_all(part, t, owners - 1, rs_send)

        wait_all(zb, t, others - 1, z_send)

        wait_all(ag, t, owners - 1, ag_recv)

        wait_all(ag, t, owners - 1, ag_send)

    device = (sa * n_sb + sb) * n_sl + sl
    group = group_rows[device // row_groups]
    block = ag[group // 2, pl.ds(group % 2 * per_half, per_half)]
    rows = jnp.concatenate([block[p] for p in range(per_half)], axis=1)
    high = rows.astype(jnp.bfloat16)
    rest = rows - high.astype(jnp.float32)
    middle = rest.astype(jnp.bfloat16)
    low = (rest - middle.astype(jnp.float32)).astype(jnp.bfloat16)
    thirds = jnp.concatenate([low, middle, high], axis=0)

    def times(k, g):
        x = jnp.dot(thirds[:, k * n:(k + 1) * n], gate[g], preferred_element_type=jnp.float32)
        return x[:RB] + x[RB:2 * RB] + x[2 * RB:]

    out[:, :n] = times(0, 0) - times(1, 1)
    out[:, n:] = times(0, 1) + times(1, 0)


def local(stem_cache, subtree_cache, final_gates, group_rows):
    stem, subtree = stem_cache[0], subtree_cache[0]
    n_sa, n_sb, n_sl = (lax.axis_size(a) for a in AXES)
    m, k = stem.shape[1:]
    n = subtree.shape[2]
    stages = m // STAGE
    owners = 4 * n_sb
    others = (n_sa // 2) * (n_sl // 2)
    count = n_sa * n_sb * n_sl
    out_rows = group_rows.shape[0] * RB // count
    dma = pltpu.SemaphoreType.DMA
    block = pl.pallas_call(
        functools.partial(kernel, n_sa, n_sb, n_sl, RB // out_rows),
        out_shape=jax.ShapeDtypeStruct((RB, 2 * n), jnp.float32),
        in_specs=[pl.BlockSpec(memory_space=pl.ANY)] * 3 + [pl.BlockSpec(memory_space=pltpu.SMEM)],
        out_specs=pl.BlockSpec(memory_space=pltpu.VMEM),
        scratch_shapes=[
            pltpu.VMEM((stages, 2, STAGE, k), jnp.bfloat16),
            pltpu.VMEM((2, k, n), jnp.bfloat16),
            pltpu.VMEM((2, n, n), jnp.bfloat16),
            pltpu.VMEM((stages, owners, RB, LANES), jnp.bfloat16),
            pltpu.VMEM((stages, owners, RB, LANES), jnp.bfloat16),
            pltpu.VMEM((stages, others, RB, LANES), jnp.float32),
            pltpu.VMEM((stages, owners, RB, LANES), jnp.float32),
            dma, dma, dma((2 * stages,)), dma((2 * stages,)),
            dma((stages,)), dma((stages,)), dma((stages,)), dma((stages,)), dma((stages,)), dma((stages,)),
        ],
        compiler_params=pltpu.CompilerParams(
            collective_id=0, has_side_effects=True, vmem_limit_bytes=60 * 1024 * 1024
        ),
    )(stem, subtree, final_gates, group_rows)
    if out_rows == RB:
        return block
    return lax.dynamic_slice_in_dim(block, lax.axis_index(AXES) * out_rows % RB, out_rows, axis=0)


def solution(mesh):
    return jax.shard_map(
        local,
        mesh=mesh,
        in_specs=(
            P(AXES, None, None, None),
            P(AXES, None, None, None),
            P(),
            P(),
        ),
        out_specs=P(AXES, None),
        check_vma=False,
    )
```

time: 139 us -> 120 us (0.86)
  Pallas kernels: 131 us -> 118 us
  local copies, waits for them, and re-layouts: 7.48 us -> 1.47 us
    pallas_call x1, Pallas kernels: 131 us -> 118 us  [local(): pl.pallas_call(functools.partial(kernel, n_sa, n_sb, n_sl, RB // out_rows...]
    unnamed x9 -> x1, local copies, waits for them, and re-layouts: 7.48 us -> 1.47 us
where the time goes in v2:
time: 120 us
  Pallas kernels  118 us (98%)
  local copies, waits for them, and re-layouts  1.47 us (1%)
    pallas_call x1, Pallas kernels, local(): pl.pallas_call(functools.partial(kernel, n_sa, n_sb, n_sl, RB // out_rows...  118 us

profile of v2, /device:TPU:0, one launch (start us, length us, event | category | flops | bytes accessed | tf_op | source)
XLA Modules:
  0.0 119.8 jit_solution(7865211635047216737)
XLA Ops:
  0.0 118.4 %shard_map.46 = f32[16,1024]{1,0:T(8,128)} custom-call(bf16[2,128,4096]{2,1,0:T(8,128)(2,1)} %bitcast.3, bf16[2,4096,512]{2,1,0:T(8,128)(2,1)} %bitcast.2, bf16[2,512,512]{2,1,0:T(8,128)(2,1)} %gates.1, s32[32]{0:T(128)} %group_rows.1), custom_call_target="tpu_custom_call" | custom-call | tf_op jit(solution)/shard_map/pallas_call | solution.py:171
  118.4 1.5 %copy.6 = f32[16,1024]{1,0:T(8,128)} copy(f32[16,1024]{1,0:T(8,128)} %shard_map.46) | data formatting | bytes 131072

commit v3 on v2

--- a/solution.py
+++ b/solution.py
@@ -12,13 +12,15 @@
 AXES = ("sa", "sb", "sl")
 STAGE = 2 * RB
 LANES = 128
+CUTS = 2
 MESH = pl.DeviceIdType.MESH
 
 
-def kernel(n_sa, n_sb, n_sl, row_groups, stem, subtree, gates, group_rows, out, held, sub, gate, part, rs, zb, ag,
+def kernel(n_sa, n_sb, n_sl, row_groups, stem, subtree, gates, group_rows, out, held, sub, gate, total, part, rs, zb, ag,
            sub_sem, gate_sem, stem_send, stem_recv, rs_send, rs_recv, z_send, z_recv, ag_send, ag_recv):
     sa, sb, sl = (lax.axis_index(a) for a in AXES)
     stages = held.shape[0]
+    depth = held.shape[3] // CUTS
     n = subtree.shape[2]
     owners = 4 * n_sb
     per_half = owners // 2
@@ -53,9 +55,11 @@
     pl.semaphore_wait(barrier, 2 + (owners - 1) + (others - 1))
 
     def stem_copy(i):
-        target = sb if i < stages else pair
-        return pltpu.make_async_remote_copy(
-            src_ref=stem.at[:, pl.ds(i * RB, RB), :], dst_ref=held.at[i // 2, :, pl.ds(i % 2 * RB, RB)],
+        t, cut = divmod(i, CUTS)
+        target = sb if t < stages // 2 else pair
+        return pltpu.make_async_remote_copy(
+            src_ref=stem.at[:, pl.ds(t * STAGE, STAGE), pl.ds(cut * depth, depth)],
+            dst_ref=held.at[t, :, :, pl.ds(cut * depth, depth)],
             send_sem=stem_send.at[i], recv_sem=stem_recv.at[i], device_id=(far, target, sl), device_id_type=MESH)
 
     def rs_copy(t, peer):
@@ -86,29 +90,28 @@
     pltpu.make_async_copy(gates, gate, gate_sem).wait()
 
     for t in range(stages):
-        for i in (2 * t, 2 * t + 1):
+        for cut in range(CUTS):
+            i = t * CUTS + cut
             stem_copy(i).wait_send()
-            if i + 2 < 2 * stages:
+            if i + 2 < CUTS * stages:
                 stem_copy(i + 2).start()
-        for i in (2 * t, 2 * t + 1):
             stem_copy(i).wait_recv()
-
-        @functools.partial(lax.fori_loop, 0, 2, init_val=0)
-        def _(i, carry, t=t):
-            cols = pl.ds(pl.multiple_of(i * (n // 2), n // 2), n // 2)
-            left = held[t].reshape(2 * STAGE, held.shape[3])
-            by_real = jnp.dot(left, sub[0, :, cols], preferred_element_type=jnp.float32)
-            by_imag = jnp.dot(left, sub[1, :, cols], preferred_element_type=jnp.float32)
-            real = (by_real[:STAGE] - by_imag[STAGE:]).astype(jnp.bfloat16)
-            imag = (by_imag[:STAGE] + by_real[STAGE:]).astype(jnp.bfloat16)
-            pieces = n // 2 // LANES
-            for half in range(2):
-                for p in range(pieces):
-                    at = half * per_half + i * pieces + p
-                    block = (slice(half * RB, (half + 1) * RB), slice(p * LANES, (p + 1) * LANES))
-                    part[t, at] = real[block]
-                    part[t, at + per_half // 2] = imag[block]
-            return carry
+            deep = slice(cut * depth, (cut + 1) * depth)
+            left = held[t, :, :, deep].reshape(2 * STAGE, depth)
+            for g in range(2):
+                product = jnp.dot(left, sub[g, deep, :], preferred_element_type=jnp.float32)
+                if cut == 0:
+                    total[g] = product
+                else:
+                    total[g] += product
+
+        real = (total[0, :STAGE] - total[1, STAGE:]).astype(jnp.bfloat16)
+        imag = (total[1, :STAGE] + total[0, STAGE:]).astype(jnp.bfloat16)
+        for half in range(2):
+            for p in range(per_half // 2):
+                block = (slice(half * RB, (half + 1) * RB), slice(p * LANES, (p + 1) * LANES))
+                part[t, half * per_half + p] = real[block]
+                part[t, half * per_half + per_half // 2 + p] = imag[block]
 
         for peer in near_peers:
             rs_copy(t, peer).start()
@@ -177,11 +180,12 @@
             pltpu.VMEM((stages, 2, STAGE, k), jnp.bfloat16),
             pltpu.VMEM((2, k, n), jnp.bfloat16),
             pltpu.VMEM((2, n, n), jnp.bfloat16),
+            pltpu.VMEM((2, 2 * STAGE, n), jnp.float32),
             pltpu.VMEM((stages, owners, RB, LANES), jnp.bfloat16),
             pltpu.VMEM((stages, owners, RB, LANES), jnp.bfloat16),
             pltpu.VMEM((stages, others, RB, LANES), jnp.float32),
             pltpu.VMEM((stages, owners, RB, LANES), jnp.float32),
-            dma, dma, dma((2 * stages,)), dma((2 * stages,)),
+            dma, dma, dma((CUTS * stages,)), dma((CUTS * stages,)),
             dma((stages,)), dma((stages,)), dma((stages,)), dma((stages,)), dma((stages,)), dma((stages,)),
         ],
         compiler_params=pltpu.CompilerParams(

time: 120 us -> 120 us (level)
  no operation moved by 1% of the time
where the time goes in v3:
time: 120 us
  Pallas kernels  118 us (98%)
  local copies, waits for them, and re-layouts  1.47 us (1%)
    pallas_call x1, Pallas kernels, local(): pl.pallas_call(functools.partial(kernel, n_sa, n_sb, n_sl, RB // out_rows...  118 us

profile of v3, /device:TPU:0, one launch (start us, length us, event | category | flops | bytes accessed | tf_op | source)
XLA Modules:
  0.0 119.6 jit_solution(14456988520007194872)
XLA Ops:
  0.0 118.1 %shard_map.46 = f32[16,1024]{1,0:T(8,128)} custom-call(bf16[2,128,4096]{2,1,0:T(8,128)(2,1)} %bitcast.3, bf16[2,4096,512]{2,1,0:T(8,128)(2,1)} %bitcast.2, bf16[2,512,512]{2,1,0:T(8,128)(2,1)} %gates.1, s32[32]{0:T(128)} %group_rows.1), custom_call_target="tpu_custom_call" | custom-call | tf_op jit(solution)/shard_map/pallas_call | solution.py:174
  118.1 1.5 %copy.6 = f32[16,1024]{1,0:T(8,128)} copy(f32[16,1024]{1,0:T(8,128)} %shard_map.46) | data formatting | bytes 131072
